TPU v7x, 128 devices: a whole 4x4x4 slice. The times are simulated.
128 devices in a mesh: ind: 8 (over z_hi, y), var: 16 (over z_lo, x, core).
Axes of the slice: x: 4, y: 4, z: 4 (z_hi: 2, z_lo: 2; z = z_hi * 2 + z_lo), core: 2. Of those that a mesh axis runs over, the one named last changes fastest.
Arguments:
- genotypes: bfloat16 [2048, 786432], P('var', 'ind'), may hold values from -6 to 6, as said below
- residual: float32 [786432], P('ind'), may hold values from -6 to 6
- ancestry: int32 [786432], P('ind'), may hold values from 0 to 4, never falling along the last dimension, each value on 1 to 393216 neighbouring positions
- effects: float32 [5, 2048], P(None, 'var'), may hold values from -4 to 4
- prior_precision: float32 [5, 5], replicated, may hold values from -12 to 12, as said below
- noise_var: float32 [5], replicated, may hold values from 0.5 to 2
- block_index: int32 [3, 512], P(None, 'var'), may hold values from 0 to 127, as said below
- gaussians: float32 [3, 5, 512], P(None, None, 'var'), may hold values from -5 to 5
Outputs:
- new_residual: float32 [786432], P(('ind', 'var'))
- new_effects: float32 [5, 2048], P(None, 'var')
Inputs may be any that keep to these rules, and one draw needn't show every extreme that they name: Scaled genotypes; variants and individuals have different scales. `prior_precision`: symmetric positive definite. `block_index`: in each step the 32 entries held by one index of var are distinct rows among that index's 128 variants; rows 0 and 127 appear in every draw.
All inputs are finite; a program needn't handle non-finite values.
Results may differ from a plain program's by a relative error of at most 0.0003.
Values sent between devices are 32-bit elements; how exact they have to be, the bound alone decides.
A program may use at most 128 MiB of HBM per device.

v0:
```python
import jax
import jax.numpy as jnp
from jax import lax
from jax.sharding import PartitionSpec as P

highest = lax.Precision.HIGHEST


def posterior_draw(scores, norm_sum, before, prior_precision, noise_var, noise_now):
    ancestries = scores.shape[0]
    inverse = 1.0 / noise_var
    target = (scores + norm_sum * before) * inverse[:, None]
    lower = [[None] * ancestries for column in range(ancestries)]
    for a in range(ancestries):
        for b in range(a + 1):
            total = prior_precision[a, b] + jnp.zeros_like(scores[0])
            if a == b:
                total = total + norm_sum[a] * inverse[a]
            for m in range(b):
                total = total - lower[a][m] * lower[b][m]
            if a == b:
                lower[a][a] = jnp.sqrt(total)
            else:
                lower[a][b] = total / lower[b][b]
    forward = []
    for a in range(ancestries):
        total = target[a]
        for m in range(a):
            total = total - lower[a][m] * forward[m]
        forward.append(total / lower[a][a] + noise_now[a])
    backward = [None] * ancestries
    for a in reversed(range(ancestries)):
        total = forward[a]
        for m in range(a + 1, ancestries):
            total = total - lower[m][a] * backward[m]
        backward[a] = total / lower[a][a]
    return jnp.stack(backward)


def per_device(
    genotypes, residual, ancestry, effects, prior_precision, noise_var, block_index, gaussians
):
    ancestries = effects.shape[0]
    row_count = residual.shape[0]
    var_size = lax.axis_size("var")
    var_index = lax.axis_index("var")
    part_rows = row_count // var_size
    onehot = (ancestry[None, :] == jnp.arange(ancestries, dtype=jnp.int32)[:, None]).astype(
        jnp.float32
    )
    columns = jnp.arange(effects.shape[1], dtype=jnp.int32)
    contract = (((1,), (1,)), ((), ()))
    current = residual
    current_effects = effects
    for s in range(block_index.shape[0]):
        picked = block_index[s]
        chosen = jnp.take(genotypes, picked, axis=0).astype(jnp.float32)
        selector = (picked[:, None] == columns[None, :]).astype(jnp.float32)
        weighted = onehot * current[None, :]
        scores = lax.dot_general(weighted, chosen, contract, precision=highest)
        norm_sum = lax.dot_general(onehot, chosen * chosen, contract, precision=highest)
        before = jnp.dot(current_effects, selector.T, precision=highest)
        noise_now = gaussians[s]
        score_all, norm_all = lax.psum((scores, norm_sum), "ind")
        drawn = posterior_draw(score_all, norm_all, before, prior_precision, noise_var, noise_now)
        change = drawn - before
        current_effects = current_effects + jnp.dot(change, selector, precision=highest)
        spread = jnp.dot(change, chosen, precision=highest)
        update = jnp.sum(onehot * spread, axis=0)
        current = current - lax.psum(update, "var")
    result_rows = lax.dynamic_slice_in_dim(current, var_index * part_rows, part_rows, 0)
    return (result_rows, current_effects)


def solution(mesh):
    return jax.shard_map(
        per_device,
        mesh=mesh,
        in_specs=(
            P("var", "ind"),
            P("ind"),
            P("ind"),
            P(None, "var"),
            P(),
            P(),
            P(None, "var"),
            P(None, None, "var"),
        ),
        out_specs=(P(("ind", "var")), P(None, "var")),
        check_vma=False,
    )
```

profile of v0, /device:TPU:1, one launch (start us, length us, event | category | flops | bytes accessed | tf_op | source)
XLA Modules:
  0.0 542.1 jit_solution(6011189813853999114)
XLA Ops:
  7.2 0.0 all-reduce.7.cloned.1.call-start
  7.2 0.8 compare_and_fusion.1
  8.0 0.8 slice_bitcast_fusion
  8.8 17.0 %gather_fusion = bf16[32,98304]{1,0:T(8,128)(2,1)} fusion(bf16[128,98304]{1,0:T(8,128)(2,1)} %param.10, s32[1024]{0:T(1024)S(1)} %pad_clamp_fusion.2), kind=kCustom, calls=%fused_computation.clone | custom fusion | bytes 12583040 | tf_op jit(solution)/shard_map/jit(_take)/gather | solution.py:57
  25.9 9.7 %fusion.6 = f32[5,32]{1,0:T(8,128)S(1)} fusion(s32[98304]{0:T(1024)S(1)} %copy-done.4, bf16[32,98304]{1,0:T(8,128)(2,1)} %gather_fusion, pred[32]{0:T(512)(128)(4,1)S(1)} %get-tuple-element.104), kind=kOutput, calls=%fused_computation.12 | convolution fusion | flops 198672384 | bytes 6685344 | tf_op jit(solution)/shard_map/dot_general | solution.py:61
  35.5 0.0 copy-done.1
  35.6 5.1 fusion.13
  40.7 0.0 copy-done.2
  40.7 0.7 fusion.53
  41.4 0.7 fusion.54
  42.1 22.6 %all-reduce.2 = (f32[5,32]{1,0:T(8,128)S(1)}, f32[5,32]{1,0:T(8,128)S(1)}) all-reduce(f32[5,32]{1,0:T(8,128)S(1)} %fusion.6, f32[5,32]{1,0:T(8,128)S(1)} %fusion.13), channel_id=1, replica_groups=mesh['ind'=8,'var'=16] {'ind'}, use_global_device_ids=true, to_apply=%region_1.3 | all-reduce | flops 320 | bytes 2560 | tf_op jit(solution)/shard_map/psum | solution.py:64
  64.7 0.2 add_multiply_fusion.2
  64.9 8.5 %bitcast_add_fusion.11 = (f32[1,32]{1,0:T(1,128)S(1)}, f32[1,32]{1,0:T(1,128)S(1)}, f32[1,32]{1,0:T(1,128)S(1)}, f32[1,32]{1,0:T(1,128)S(1)}, f32[1,32]{1,0:T(1,...) fusion(f32[3,5,32]{2,0,1:T(4,128)S(1)} %copy-done.3, ...), kind=kLoop, calls=%fused_computation.88 | loop fusion | flops 1728 | bytes 3384 | tf_op jit(solution)/shard_map/add | solution.py:30
  73.4 2.4 subtract_divide_fusion.24
  75.8 1.3 subtract_divide_fusion.20
  77.1 8.7 %fusion.27 = f32[98304]{0:T(1024)} fusion(s32[98304]{0:T(1024)S(1)} %copy-done.4, f32[5,32]{1,0:T(8,128)S(1)} %stack.6, f32[5,32]{1,0:T(8,128)S(1)} %get-tuple-element.112, bf16[32,98304]{1,0:T(8,128)(2,1)} %gather_fusion, pred[32]{0:T(512)(128)(4,1)S(1)} %get-tuple-element.104), kind=kOutput, calls=%fused_computation.37 | convolution fusion | flops 193265824 | bytes 7079200 | tf_op jit(solution)/shard_map/dot_general | solution.py:68
  85.7 0.0 all-reduce.7.cloned.1.call-update
  85.8 0.3 all-reduce.9.cloned.1.call-start
  86.0 17.2 %gather_fusion.1 = bf16[32,98304]{1,0:T(8,128)(2,1)} fusion(bf16[128,98304]{1,0:T(8,128)(2,1)} %param.10, s32[1024]{0:T(1024)S(1)} %pad_clamp_fusion.1), kind=kCustom, calls=%fused_computation.1.clone | custom fusion | bytes 12583040 | tf_op jit(solution)/shard_map/jit(_take)/gather | solution.py:57
  103.3 9.8 %fusion.3 = f32[5,32]{1,0:T(8,128)S(1)} fusion(s32[98304]{0:T(1024)S(1)} %copy-done.4, bf16[32,98304]{1,0:T(8,128)(2,1)} %gather_fusion.1, pred[32]{0:T(512)(128)(4,1)S(1)} %get-tuple-element.55), kind=kOutput, calls=%fused_computation.9 | convolution fusion | flops 198672384 | bytes 6685344 | tf_op jit(solution)/shard_map/dot_general | solution.py:61
  113.1 17.4 %gather_fusion.2 = bf16[32,98304]{1,0:T(8,128)(2,1)} fusion(bf16[128,98304]{1,0:T(8,128)(2,1)} %param.10, s32[1024]{0:T(1024)S(1)} %pad_clamp_fusion), kind=kCustom, calls=%fused_computation.2.clone | custom fusion | bytes 12583040 | tf_op jit(solution)/shard_map/jit(_take)/gather | solution.py:57
  130.4 0.2 convolution_add_fusion.2
  130.6 73.2 %all-reduce.7.cloned.1.call-done = f32[98304]{0:T(1024)} async-done(((f32[98304]{0:T(1024)}), f32[98304]{0:T(1024)}) %all-reduce.7.cloned.1.call-update) | async-done | bytes 393232 | tf_op jit(solution)/shard_map/psum | solution.py:70
  203.8 1.0 sub.929
  204.8 7.1 %fusion.11 = f32[5,32]{1,0:T(8,128)S(1)} fusion(f32[98304]{0:T(1024)S(1)} %sub.929, s32[98304]{0:T(1024)S(1)} %copy-done.4, bf16[32,98304]{1,0:T(8,128)(2,1)} %gather_fusion.1, pred[32]{0:T(512)(128)(4,1)S(1)} %get-tuple-element.55), kind=kOutput, calls=%fused_computation.20 | convolution fusion | flops 192872448 | bytes 7078560 | tf_op jit(solution)/shard_map/dot_general | solution.py:60
  212.0 20.5 %all-reduce.1 = (f32[5,32]{1,0:T(8,128)S(1)}, f32[5,32]{1,0:T(8,128)S(1)}) all-reduce(f32[5,32]{1,0:T(8,128)S(1)} %fusion.3, f32[5,32]{1,0:T(8,128)S(1)} %fusion.11), channel_id=1, replica_groups=mesh['ind'=8,'var'=16] {'ind'}, use_global_device_ids=true, to_apply=%region_5.7 | all-reduce | flops 320 | bytes 2560 | tf_op jit(solution)/shard_map/psum | solution.py:64
  232.5 0.2 add_multiply_fusion.1
  232.7 8.5 %bitcast_add_fusion.6 = (f32[1,32]{1,0:T(1,128)S(1)}, f32[1,32]{1,0:T(1,128)S(1)}, f32[1,32]{1,0:T(1,128)S(1)}, f32[1,32]{1,0:T(1,128)S(1)}, f32[1,32]{1,0:T(1,1...) fusion(f32[3,5,32]{2,0,1:T(4,128)S(1)} %copy-done.3, ...), kind=kLoop, calls=%fused_computation.82 | loop fusion | flops 1728 | bytes 3384 | tf_op jit(solution)/shard_map/add | solution.py:30
  241.2 2.4 subtract_divide_fusion.14
  243.6 1.3 subtract_divide_fusion.10
  244.9 8.8 %fusion.28 = f32[98304]{0:T(1024)} fusion(s32[98304]{0:T(1024)S(1)} %copy-done.4, f32[5,32]{1,0:T(8,128)S(1)} %stack.7, f32[5,32]{1,0:T(8,128)S(1)} %get-tuple-element.114, bf16[32,98304]{1,0:T(8,128)(2,1)} %gather_fusion.1, pred[32]{0:T(512)(128)(4,1)S(1)} %get-tuple-element.55), kind=kOutput, calls=%fused_computation.38 | convolution fusion | flops 193265824 | bytes 7079200 | tf_op jit(solution)/shard_map/dot_general | solution.py:68
  253.7 0.0 all-reduce.9.cloned.1.call-update
  253.7 0.0 all-reduce.11.cloned.1.call-start
  253.8 9.4 %fusion = f32[5,32]{1,0:T(8,128)S(1)} fusion(s32[98304]{0:T(1024)S(1)} %copy-done.4, bf16[32,98304]{1,0:T(8,128)(2,1)} %gather_fusion.2, pred[32]{0:T(512)(128)(4,1)S(1)} %get-tuple-element.102), kind=kOutput, calls=%fused_computation.6 | convolution fusion | flops 198672384 | bytes 6685344 | tf_op jit(solution)/shard_map/dot_general | solution.py:61
  263.1 0.2 convolution_add_fusion.1
  263.3 105.7 %all-reduce.9.cloned.1.call-done = f32[98304]{0:T(1024)} async-done(((f32[98304]{0:T(1024)}), f32[98304]{0:T(1024)}) %all-reduce.9.cloned.1.call-update) | async-done | bytes 393232 | tf_op jit(solution)/shard_map/psum | solution.py:70
  369.0 1.0 sub.971
  370.0 7.1 %fusion.9 = f32[5,32]{1,0:T(8,128)S(1)} fusion(f32[98304]{0:T(1024)S(1)} %sub.971, s32[98304]{0:T(1024)S(1)} %copy-done.4, bf16[32,98304]{1,0:T(8,128)(2,1)} %gather_fusion.2, pred[32]{0:T(512)(128)(4,1)S(1)} %get-tuple-element.102), kind=kOutput, calls=%fused_computation.18 | convolution fusion | flops 192872448 | bytes 7078560 | tf_op jit(solution)/shard_map/dot_general | solution.py:60
  377.2 20.5 %all-reduce = (f32[5,32]{1,0:T(8,128)S(1)}, f32[5,32]{1,0:T(8,128)S(1)}) all-reduce(f32[5,32]{1,0:T(8,128)S(1)} %fusion, f32[5,32]{1,0:T(8,128)S(1)} %fusion.9), channel_id=1, replica_groups=mesh['ind'=8,'var'=16] {'ind'}, use_global_device_ids=true, to_apply=%region_9.11 | all-reduce | flops 320 | bytes 2560 | tf_op jit(solution)/shard_map/psum | solution.py:64
  397.7 0.2 add_multiply_fusion
  397.9 8.5 %bitcast_add_fusion.1 = (f32[1,32]{1,0:T(1,128)S(1)}, f32[1,32]{1,0:T(1,128)S(1)}, f32[1,32]{1,0:T(1,128)S(1)}, f32[1,32]{1,0:T(1,128)S(1)}, f32[1,32]{1,0:T(1,1...) fusion(f32[3,5,32]{2,0,1:T(4,128)S(1)} %copy-done.3, ...), kind=kLoop, calls=%fused_computation.76 | loop fusion | flops 1728 | bytes 3384 | tf_op jit(solution)/shard_map/add | solution.py:30
  406.4 2.4 subtract_divide_fusion.4
  408.8 1.3 subtract_divide_fusion
  410.1 8.6 %fusion.29 = f32[98304]{0:T(1024)} fusion(s32[98304]{0:T(1024)S(1)} %copy-done.4, f32[5,32]{1,0:T(8,128)S(1)} %stack.8, f32[5,32]{1,0:T(8,128)S(1)} %get-tuple-element.116, bf16[32,98304]{1,0:T(8,128)(2,1)} %gather_fusion.2, pred[32]{0:T(512)(128)(4,1)S(1)} %get-tuple-element.102), kind=kOutput, calls=%fused_computation.39 | convolution fusion | flops 193265824 | bytes 7079200 | tf_op jit(solution)/shard_map/dot_general | solution.py:68
  418.7 0.0 all-reduce.11.cloned.1.call-update
  418.7 0.8 convolution_add_fusion
  419.5 114.5 %all-reduce.11.cloned.1.call-done = f32[98304]{0:T(1024)} async-done(((f32[98304]{0:T(1024)}), f32[98304]{0:T(1024)}) %all-reduce.11.cloned.1.call-update) | async-done | bytes 393232 | tf_op jit(solution)/shard_map/psum | solution.py:70
  534.1 1.3 dynamic-slice_subtract_fusion
  (19 shorter events, 0.1 us)
Async XLA Ops:
  7.2 196.6 %all-reduce.7.cloned.1.call-start = ((), (), s32[]{:S(2)}) async-start(), calls=%async_computation | async-start | bytes 786432 | tf_op jit(solution)/shard_map/psum | solution.py:70
  8.8 17.0 %copy-start.4 = (s32[98304]{0:T(1024)S(1)}, s32[98304]{0:T(1024)}, u32[]{:S(2)}) copy-start(s32[98304]{0:T(1024)} %param.12) | copy-start | bytes 1179652
  25.9 9.7 %copy-start = (bf16[32,98304]{1,0:T(8,128)(2,1)S(1)}, bf16[32,98304]{1,0:T(8,128)(2,1)}, u32[]{:S(2)}) copy-start(bf16[32,98304]{1,0:T(8,128)(2,1)} %gather_fusion) | copy-start | bytes 18874372
  25.9 9.7 %copy-start.1 = (f32[98304]{0:T(1024)S(1)}, f32[98304]{0:T(1024)}, u32[]{:S(2)}) copy-start(f32[98304]{0:T(1024)} %param.11) | copy-start | bytes 1179652
  35.6 5.1 copy-start.6
  35.6 5.1 copy-start.2
  35.6 29.1 %copy-start.5 = (f32[5,128]{1,0:T(8,128)S(1)}, f32[5,128]{1,0:T(8,128)}, u32[]{:S(2)}) copy-start(f32[5,128]{1,0:T(8,128)} %param.13) | copy-start | bytes 7684
  35.6 29.3 %copy-start.3 = (f32[3,5,32]{2,0,1:T(4,128)S(1)}, f32[3,5,32]{2,0,1:T(4,128)}, u32[]{:S(2)}) copy-start(f32[3,5,32]{2,0,1:T(4,128)} %param.17) | copy-start | bytes 5764
  85.8 283.2 %all-reduce.9.cloned.1.call-start = ((), (), s32[]{:S(2)}) async-start(), calls=%async_computation.1 | async-start | bytes 786432 | tf_op jit(solution)/shard_map/psum | solution.py:70
  253.7 280.3 %all-reduce.11.cloned.1.call-start = ((), (), s32[]{:S(2)}) async-start(), calls=%async_computation.2 | async-start | bytes 786432 | tf_op jit(solution)/shard_map/psum | solution.py:70
Sparse Core Ops, SparseCore 0:
  85.9 117.8 all-reduce.6
  253.8 115.0 all-reduce.8
  418.8 115.1 all-reduce.10
where the time goes:
time: 550 us; the launch traced here: 542 us
  waiting for transfers between devices  293 us (53%)
  matrix products  76.1 us (14%)
  blocking collectives  63.6 us (12%)
  local copies, waits for them, and re-layouts  53.9 us (10%)
  other arithmetic  40.7 us (7%)
  between operations  14.1 us (3%)
    psum x3, waiting for transfers between devices, per_device(): current = current - lax.psum(update, 'var')  293 us
    psum x3, blocking collectives, per_device(): score_all, norm_all = lax.psum((scores, norm_sum), 'ind')  63.6 us
    gather x3, local copies, waits for them, and re-layouts, per_device(): chosen = jnp.take(genotypes, picked, axis=0).astype(jnp.float32)  51.6 us
    dot_general x3, matrix products, per_device(): lax.dot_general(onehot, chosen * chosen, contract, precision=highest)  28.8 us
    dot_general x3, matrix products, per_device(): spread = jnp.dot(change, chosen, precision=highest)  26.1 us
    add x3, other arithmetic, posterior_draw(): forward.append(total / lower[a][a] + noise_now[a])  25.5 us
    dot_general x3, matrix products, per_device(): scores = lax.dot_general(weighted, chosen, contract, precision=highest)  19.3 us
  transfers between devices with their start and end apart: 3, of which 3 were waited for; matrix products, arithmetic and copies ran while one was open for 10% of the time, Pallas kernels for 0%

commit v1 on v0

v1 whole, which is shorter than its diff:
```python
import functools

import jax
import jax.numpy as jnp
from jax import lax
from jax.experimental import pallas as pl
from jax.experimental.pallas import tpu as pltpu
from jax.sharding import PartitionSpec as P

MESH = pl.DeviceIdType.MESH
HIGHEST = lax.Precision.HIGHEST
F32 = jnp.float32

K = 5
ROWS = 128
BV = 32
STEPS = 3
NJ = 96
TJ = 6
NS = NJ // TJ
CJ = 3
NCH = NJ // CJ
NBUF = 6
N_IND = 8
FAR_FIRST = (6, 2, 5, 7, 4, 1, 3)
NEAR_FIRST = (1, 3, 4, 5, 7, 2, 6)


def far_first(m):
    return (2 + 3 * m + 3 * (m * (m - 1) // 2)) % 4


def kernel(
    g_hbm, r_hbm, places, eff_in, prior, noise, rows, rows_v, gauss,
    out_r, out_eff,
    wide, stage, r, eff, prefix, norm_prefix, part, spots, table, fix,
    norm_part, norm_span, factors, changes,
    core_send, core_recv, far_send, far_recv, norm_recv, ind_recv,
    load_sem, in_sem, core_ss, core_rs, far_ss, far_rs, ag_ss, ag_rs, fw_ss, fw_rs, nrm_ss, nrm_rs, ind_ss, ind_rs,
):
    ind, var = lax.axis_index("ind"), lax.axis_index("var")
    core, chip = var % 2, var // 2
    x, z = chip % 4, chip // 4
    y, zh = ind % 4, ind // 4
    partner = var + 1 - 2 * core

    def chip_at(o, sign):
        return ((z + o // 4) % 2) * 4 + (x + sign * (o % 4) + 4) % 4

    def ind_at(o):
        return ((zh + o // 4) % 2) * 4 + (y + o % 4) % 4

    def slice_tiles(w):
        return pl.ds(w * TJ, TJ)

    def remote(src, dst, send, recv, to):
        return pltpu.make_async_remote_copy(
            src_ref=src, dst_ref=dst, send_sem=send, recv_sem=recv, device_id=to, device_id_type=MESH
        )

    def chunk(c, slot):
        at = pl.multiple_of(c * CJ * 1024, CJ * 1024)
        return pltpu.make_async_copy(g_hbm.at[:, pl.ds(at, CJ * 1024)], stage.at[slot], load_sem.at[slot])

    def core_copy(o):
        return remote(core_send.at[o], core_recv.at[o], core_ss.at[o], core_rs.at[o], (ind, partner))

    def far_copy(o):
        return remote(
            far_send.at[o], far_recv.at[o], far_ss.at[o], far_rs.at[o], (ind, chip_at(o, 1) * 2 + core)
        )

    def gather_copy(o):
        own = slice_tiles(var)
        return remote(r.at[own], r.at[own], ag_ss.at[o], ag_rs.at[o], (ind, chip_at(o, 1) * 2 + core))

    def forward_copy(o):
        at = slice_tiles(chip_at(o, -1) * 2 + core)
        return remote(r.at[at], r.at[at], fw_ss.at[o], fw_rs.at[o], (ind, partner))

    def norm_copy(o):
        return remote(norm_recv.at[ind], norm_recv.at[ind], nrm_ss.at[o], nrm_rs.at[o], (ind_at(o), var))

    def ind_copy(s, o):
        return remote(ind_recv.at[s, ind], ind_recv.at[s, ind], ind_ss.at[s, o], ind_rs.at[s, o], (ind_at(o), var))

    r_copy = pltpu.make_async_copy(r_hbm, r, in_sem)
    r_copy.start()
    for c in range(NBUF):
        chunk(c, c).start()

    barrier = pltpu.get_barrier_semaphore()
    pl.semaphore_signal(barrier, inc=1, device_id=(ind, partner), device_id_type=MESH)
    for o in range(1, 8):
        pl.semaphore_signal(barrier, inc=1, device_id=(ind, chip_at(o, 1) * 2 + core), device_id_type=MESH)
    for o in range(1, N_IND):
        pl.semaphore_signal(barrier, inc=1, device_id=(ind_at(o), var), device_id_type=MESH)

    r_copy.wait()
    eff[...] = jnp.zeros_like(eff)
    eff[0:K, :] = eff_in[...]

    lanes = lax.broadcasted_iota(jnp.int32, (8, 128), 1)
    place = lax.broadcasted_iota(jnp.int32, (8, 128), 0) * 128 + lanes

    wide_rows = wide.reshape(NJ * ROWS * 8, 128)

    def tile(j, row):
        return wide[j * ROWS + row]

    def score_slice(s, q):
        held = [r[q * TJ + t] for t in range(TJ)]
        for c in range(BV):
            row = rows[s, c]
            total = prefix[q, c]
            for t in range(TJ):
                total = total + held[t] * tile(q * TJ + t, row)
            prefix[q + 1, c] = total

    prefix[0] = jnp.zeros_like(prefix[0])

    def load(q, norm):
        for h in range(TJ // CJ):
            c = q * (TJ // CJ) + h
            slot = lax.rem(c, NBUF)
            chunk(c, slot).wait()
            norm_prefix[c] = norm

            def widen(jj, norm):
                sums = [norm[a * 16 : (a + 1) * 16] for a in range(8)]
                for t in range(8):
                    at = pl.multiple_of(jj * 1024 + t * 128, 128)
                    for a in range(8):
                        v = stage[slot, a * 16 : (a + 1) * 16, pl.ds(at, 128)].astype(F32)
                        wide_rows[pl.ds((c * CJ + jj) * (ROWS * 8) + a * 128 + t, 16, stride=8), :] = v
                        sums[a] = sums[a] + v * v
                return jnp.concatenate(sums, axis=0)

            norm = lax.fori_loop(0, CJ, widen, norm)

            @pl.when(c + NBUF < NCH)
            def _():
                chunk(c + NBUF, slot).start()

        score_slice(0, q)
        return norm

    norm_all = lax.fori_loop(0, NS, load, jnp.zeros((ROWS, 128), F32))

    def pick_row(k, width):
        return (lax.broadcasted_iota(jnp.int32, (8, width), 0) == k).astype(F32)

    contract_last = (((1,), (1,)), ((), ()))

    def lane_sums(values):
        total = jnp.zeros((8, values[0].shape[0]), F32)
        for k in range(K):
            total = total + lax.dot_general(
                pick_row(k, 128), values[k], contract_last, precision=HIGHEST, preferred_element_type=F32
            )
        return total

    norm_span[K - 1] = jnp.zeros((ROWS, 128), F32)

    def norm_below(b, carry):
        c = places[16 + b]
        p = places[20 + b]
        keep = [t * 1024 + place < p for t in range(CJ)]

        def some_rows(a, carry):
            for i in range(8):
                total = jnp.zeros((8, 128), F32)
                for t in range(CJ):
                    v = tile(c * CJ + t, a * 8 + i)
                    total = total + jnp.where(keep[t], v * v, 0.0)
                norm_part[i * 8 : (i + 1) * 8, :] = total
            at = pl.ds(pl.multiple_of(a * 8, 8), 8)
            here = norm_prefix[c, at, :]
            for sub in range(8):
                here = here + norm_part[pl.ds(sub, 8, stride=8), :]
            norm_span[b, at, :] = here - norm_span[K - 1, at, :]
            norm_span[K - 1, at, :] = here
            return carry

        return lax.fori_loop(0, ROWS // 8, some_rows, carry)

    lax.fori_loop(0, K - 1, norm_below, 0)
    norm_recv[ind] = lane_sums([norm_span[k] for k in range(K - 1)] + [norm_all - norm_span[K - 1]])
    pl.semaphore_wait(barrier, 15)
    for o in range(1, N_IND):
        norm_copy(o).start()

    def send_scores(s):
        spots[...] = jnp.zeros_like(spots)

        def below(b, carry):
            q = places[24 + b]
            p = places[28 + b]
            held = []
            for t in range(TJ):
                held.append(jnp.where(t * 1024 + place < p, r[q * TJ + t], 0.0))
            for c in range(BV):
                row = rows[s, c]
                total = prefix[q, c]
                for t in range(TJ):
                    total = total + held[t] * tile(q * TJ + t, row)
                part[pl.ds(pl.multiple_of((b * BV + c) * 8, 8), 8), :] = total - spots[c]
                spots[c] = total
            return carry

        lax.fori_loop(0, K - 1, below, 0)
        for c in range(BV):
            at = ((K - 1) * BV + c) * 8
            part[at : at + 8, :] = prefix[NS, c] - spots[c]
        values = []
        for k in range(K):
            groups = []
            for a in range(BV // 8):
                total = part[pl.ds((k * BV + a * 8) * 8, 8, stride=8), :]
                for sub in range(1, 8):
                    total = total + part[pl.ds((k * BV + a * 8) * 8 + sub, 8, stride=8), :]
                groups.append(total)
            values.append(jnp.concatenate(groups, axis=0))
        ind_recv[s, ind] = jnp.concatenate([lane_sums(values), jnp.zeros((8, 128 - BV), F32)], axis=1)
        for o in range(1, N_IND):
            ind_copy(s, o).start()

    send_scores(0)

    inverse = [1.0 / jnp.full((1, BV), noise[k], F32) for k in range(K)]

    def selector(s):
        return (lax.broadcasted_iota(jnp.int32, (ROWS, BV), 0) == rows_v[pl.ds(s, 1), :]).astype(F32)

    def entry(a, b):
        return a * (a + 1) // 2 + b

    n_entries = entry(K, 0)

    for o in range(1, N_IND):
        norm_copy(o).wait_recv()
    norm_total = norm_recv[0]
    for other in range(1, N_IND):
        norm_total = norm_total + norm_recv[other]

    def factor(s, carry):
        norm = jnp.dot(norm_total, selector(s), precision=HIGHEST, preferred_element_type=F32)
        lower = [[None] * K for a in range(K)]
        scale = [None] * K
        for a in range(K):
            for b in range(a + 1):
                total = jnp.full((1, BV), prior[a, b], F32)
                if a == b:
                    total = total + norm[a : a + 1] * inverse[a]
                for m in range(b):
                    total = total - lower[a][m] * lower[b][m]
                if a == b:
                    scale[a] = 1.0 / jnp.sqrt(total)
                    lower[a][a] = scale[a]
                else:
                    lower[a][b] = total * scale[b]
                factors[s, entry(a, b) : entry(a, b) + 1, :] = lower[a][b]
        for k in range(K):
            factors[s, n_entries + k : n_entries + k + 1, :] = norm[k : k + 1]
        return carry

    lax.fori_loop(0, STEPS, factor, 0)

    def step(s, carry):
        chosen = selector(s)
        before = jnp.dot(eff[...], chosen, precision=HIGHEST, preferred_element_type=F32)
        for o in range(1, N_IND):
            ind_copy(s, o).wait_recv()
        scores = ind_recv[s, 0]
        for other in range(1, N_IND):
            scores = scores + ind_recv[s, other]
        scores = scores[:, 0:BV]

        def lower(a, b):
            return factors[s, entry(a, b) : entry(a, b) + 1, :]

        forward = []
        for a in range(K):
            norm = factors[s, n_entries + a : n_entries + a + 1, :]
            total = (scores[a : a + 1] + norm * before[a : a + 1]) * inverse[a]
            for m in range(a):
                total = total - lower(a, m) * forward[m]
            forward.append(total * lower(a, a) + gauss[s, a : a + 1, :])
        drawn = [None] * K
        for a in reversed(range(K)):
            total = forward[a]
            for m in range(a + 1, K):
                total = total - lower(m, a) * drawn[m]
            drawn[a] = total * lower(a, a)
        rest = jnp.zeros((8 - K, BV), F32)
        change = jnp.concatenate([drawn[k] - before[k : k + 1] for k in range(K)] + [rest], axis=0)
        changes[...] = change

        def splat(k, carry):
            line = changes[pl.ds(k, 1), :]
            for c in range(BV):
                table[k * BV + c] = jnp.broadcast_to(line[:, c : c + 1], (8, 128))
            return carry

        lax.fori_loop(0, K, splat, 0)
        eff[...] = eff[...] + lax.dot_general(
            change, chosen, contract_last, precision=HIGHEST, preferred_element_type=F32
        )

        def fixes(b, carry):
            q = places[24 + b]
            p = places[32 + b]
            totals = [jnp.zeros((8, 128), F32)] * TJ
            for c in range(BV):
                row = rows[s, c]
                more = table[(b + 1) * BV + c] - table[b * BV + c]
                for t in range(TJ):
                    totals[t] = totals[t] + more * tile(q * TJ + t, row)
            for t in range(TJ):
                fix[b, t] = jnp.where(t * 1024 + place >= p, totals[t], 0.0)
            return carry

        lax.fori_loop(0, K - 1, fixes, 0)

        def spread(n, carry):
            half, m = n // 8, n % 8
            o = (1 - m % 2) * 4 + far_first(m // 2)
            q = chip_at(o, 1) * 2 + core * half + (1 - core) * (1 - half)
            k = places[q]
            totals = [jnp.zeros((8, 128), F32)] * TJ
            for c in range(BV):
                row = rows[s, c]
                factor_c = table[k * BV + c]
                for t in range(TJ):
                    totals[t] = totals[t] + factor_c * tile(q * TJ + t, row)
            for b in range(K - 1):
                here = jnp.full((8, 128), places[24 + b], jnp.int32) == q
                for t in range(TJ):
                    totals[t] = totals[t] + jnp.where(here, fix[b, t], 0.0)
            mine = jnp.stack(totals)

            @pl.when(n < 8)
            def _():
                core_send[o] = mine
                core_copy(o).start()

            @pl.when(n >= 8)
            def _():
                core_copy(o).wait_recv()
                far_send[o] = mine + core_recv[o]

                @pl.when(n < 15)
                def _():
                    far_copy(o).start()

            return carry

        lax.fori_loop(0, 16, spread, 0)
        mine = far_send[0]
        for o in NEAR_FIRST:
            far_copy(o).wait_recv()
            mine = mine + far_recv[o]
        own = slice_tiles(var)
        r[own] = r[own] - mine

        @pl.when(s < STEPS - 1)
        def _():
            for o in FAR_FIRST:
                gather_copy(o).start()
            forward_copy(0).start()
            for o in NEAR_FIRST:
                gather_copy(o).wait_recv()
                forward_copy(o).start()
            for o in range(8):
                forward_copy(o).wait_recv()

            def sweep(q, carry):
                score_slice(s + 1, q)
                return carry

            lax.fori_loop(0, NS, sweep, 0)
            send_scores(s + 1)
            for o in range(8):
                forward_copy(o).wait_send()
            for o in FAR_FIRST:
                gather_copy(o).wait_send()

        for o in range(1, N_IND):
            ind_copy(s, o).wait_send()
        for o in range(8):
            core_copy(o).wait_send()
        for o in FAR_FIRST:
            far_copy(o).wait_send()
        return carry

    lax.fori_loop(0, STEPS, step, 0)
    out_r[...] = r[slice_tiles(var)]
    out_eff[...] = eff[0:K, :]
    for o in range(1, N_IND):
        norm_copy(o).wait_send()


def find_places(anc, places):
    totals = [jnp.zeros((8, 128), jnp.int32)] * (K - 1)
    for j in range(NJ):
        a = anc[j]
        totals = [t + (a < b + 1).astype(jnp.int32) for b, t in enumerate(totals)]
    begins = [jnp.sum(t) for t in totals]
    for q in range(NS):
        places[q] = sum([(begins[b] <= q * (TJ * 1024)).astype(jnp.int32) for b in range(K - 1)])
    for b in range(K - 1):
        c = jnp.minimum(lax.div(begins[b], CJ * 1024), NCH - 1)
        q = jnp.minimum(lax.div(begins[b], TJ * 1024), NS - 1)
        inside = begins[b] - q * (TJ * 1024)
        places[16 + b] = c
        places[20 + b] = begins[b] - c * (CJ * 1024)
        places[24 + b] = q
        places[28 + b] = inside
        places[32 + b] = jnp.where(inside > 0, inside, TJ * 1024)


def per_device(genotypes, residual, ancestry, effects, prior_precision, noise_var, block_index, gaussians):
    whole = pl.BlockSpec(memory_space=pltpu.VMEM)
    scalar = pl.BlockSpec(memory_space=pltpu.SMEM)
    anywhere = pl.BlockSpec(memory_space=pl.ANY)
    dma = pltpu.SemaphoreType.DMA
    places = pl.pallas_call(
        find_places,
        name="find_places",
        out_shape=jax.ShapeDtypeStruct((36,), jnp.int32),
        in_specs=[whole],
        out_specs=scalar,
    )(ancestry.reshape(NJ, 8, 128))
    new, new_effects = pl.pallas_call(
        kernel,
        name="gibbs",
        out_shape=(jax.ShapeDtypeStruct((TJ, 8, 128), F32), jax.ShapeDtypeStruct((K, ROWS), F32)),
        in_specs=[anywhere, anywhere, scalar, whole, scalar, scalar, scalar, whole, whole],
        out_specs=(whole, whole),
        scratch_shapes=[
            pltpu.VMEM((NJ * ROWS, 8, 128), F32),
            pltpu.VMEM((NBUF, ROWS, CJ * 1024), jnp.bfloat16),
            pltpu.VMEM((NJ, 8, 128), F32),
            pltpu.VMEM((8, ROWS), F32),
            pltpu.VMEM((NS + 1, BV, 8, 128), F32),
            pltpu.VMEM((NCH, ROWS, 128), F32),
            pltpu.VMEM((K * BV * 8, 128), F32),
            pltpu.VMEM((BV, 8, 128), F32),
            pltpu.VMEM((K * BV, 8, 128), F32),
            pltpu.VMEM((K - 1, TJ, 8, 128), F32),
            pltpu.VMEM((64, 128), F32),
            pltpu.VMEM((K, ROWS, 128), F32),
            pltpu.VMEM((STEPS, 24, BV), F32),
            pltpu.VMEM((8, BV), F32),
            pltpu.VMEM((8, TJ, 8, 128), F32),
            pltpu.VMEM((8, TJ, 8, 128), F32),
            pltpu.VMEM((8, TJ, 8, 128), F32),
            pltpu.VMEM((8, TJ, 8, 128), F32),
            pltpu.VMEM((N_IND, 8, 128), F32),
            pltpu.VMEM((STEPS, N_IND, 8, 128), F32),
            dma((NBUF,)),
            dma,
            dma((8,)),
            dma((8,)),
            dma((8,)),
            dma((8,)),
            dma((8,)),
            dma((8,)),
            dma((8,)),
            dma((8,)),
            dma((N_IND,)),
            dma((N_IND,)),
            dma((STEPS, N_IND)),
            dma((STEPS, N_IND)),
        ],
        compiler_params=pltpu.CompilerParams(
            vmem_limit_bytes=63 * 1024 * 1024, collective_id=0, has_side_effects=True
        ),
    )(
        genotypes,
        residual.reshape(NJ, 8, 128),
        places,
        effects,
        prior_precision,
        noise_var,
        block_index,
        block_index,
        gaussians,
    )
    return new.reshape(-1), new_effects


def solution(mesh):
    return jax.shard_map(
        per_device,
        mesh=mesh,
        in_specs=(
            P("var", "ind"),
            P("ind"),
            P("ind"),
            P(None, "var"),
            P(),
            P(),
            P(None, "var"),
            P(None, None, "var"),
        ),
        out_specs=(P(("ind", "var")), P(None, "var")),
        check_vma=False,
    )
```

time: 550 us -> 90.3 us (0.16); the launches traced: 542 us -> 90 us
  waiting for transfers between devices: 293 us -> 0 us
  Pallas kernels: 0 us -> 85.4 us
  matrix products: 76.1 us -> 0 us
  blocking collectives: 63.6 us -> 0 us
  local copies, waits for them, and re-layouts: 53.9 us -> 3.92 us
  other arithmetic: 40.7 us -> 0 us
  between operations: 14.1 us -> 0.65 us
    psum x3 -> x0, waiting for transfers between devices: 293 us -> none  [per_device(): current = current - lax.psum(update, 'var')]
    pallas_call x0 -> x2, Pallas kernels: none -> 85.4 us  [the longest x1 83.4 us: per_device(): pl.pallas_call(kernel, name='gibbs', out_shape=(jax.ShapeDtypeStruct((TJ,...]
    dot_general x15 -> x0, matrix products: 76.1 us -> none  [the longest x3 28.8 us: per_device(): lax.dot_general(onehot, chosen * chosen, contract, precision=highest)]
    psum x3 -> x0, blocking collectives: 63.6 us -> none  [per_device(): score_all, norm_all = lax.psum((scores, norm_sum), 'ind')]
    gather x3 -> x0, local copies, waits for them, and re-layouts: 51.6 us -> none  [per_device(): chosen = jnp.take(genotypes, picked, axis=0).astype(jnp.float32)]
    add x3 -> x0, other arithmetic: 25.5 us -> none  [posterior_draw(): forward.append(total / lower[a][a] + noise_now[a])]
    div x7 -> x0, other arithmetic: 11 us -> none  [the longest x3 7.16 us: posterior_draw(): lower[a][b] = total / lower[b][b]]
  transfers between devices with their start and end apart: 3 -> 0, of which waited for: 3 -> 0; matrix products, arithmetic and copies ran while one was open for 10% -> 0% of each run, Pallas kernels for 0% -> 0%
where the time goes in v1:
time: 90.3 us; the launch traced here: 90 us
  Pallas kernels  85.4 us (95%)
  local copies, waits for them, and re-layouts  3.92 us (4%)
    pallas_call x1, Pallas kernels, per_device(): pl.pallas_call(kernel, name='gibbs', out_shape=(jax.ShapeDtypeStruct((TJ,...  83.4 us
    unnamed x3, local copies, waits for them, and re-layouts  3.92 us
    pallas_call x1, Pallas kernels, per_device(): pl.pallas_call(find_places, name='find_places', out_shape=jax.ShapeDtypeS...  1.93 us

profile of v1, /device:TPU:1, one launch (start us, length us, event | category | flops | bytes accessed | tf_op | source)
XLA Modules:
  0.0 90.0 jit_solution(3409171757285396094)
XLA Ops:
  0.6 1.9 %find_places.1.places = s32[36]{0:T(128)} custom-call(s32[96,8,128]{2,1,0:T(8,128)} %bitcast.3), custom_call_target="tpu_custom_call" | custom-call | tf_op jit(solution)/shard_map/find_places/pallas_call | solution.py:427
  2.6 1.3 %copy.10.gauss = f32[3,5,32]{2,1,0:T(8,128)} copy(f32[3,5,32]{2,0,1:T(4,128)} %param.15) | data formatting | bytes 3840 | tf_op args[7]
  3.9 83.4 %gibbs.1 = (f32[6,8,128]{2,1,0:T(8,128)}, f32[5,128]{1,0:T(8,128)}) custom-call(bf16[128,98304]{1,0:T(8,128)(2,1)} %g_hbm.1, f32[96,8,128]{2,1,0:T(8,128)} %bitcast.4, s32[36]{0:T(128)} %find_places.1.places, f32[5,128]{1,0:T(8,128)} %eff_in.1, f32[5,5]{1,0:T(8,128)} %prior.1, f32[5]{0:T(128)} %noise.1, s32[3,32]{1,0:T(4,128)} %rows_v.1, s32[3,32]{1,0:T(4,128)} %rows_v.1, ...), custom_call_target="tpu_custom_call" | custom-call | tf_op jit(solution)/shard_map/gibbs/pallas_call | solution.py:434
  87.3 1.3 %copy.13 = f32[6144]{0:T(1024)} copy(f32[6144]{0:T(1024)} %bitcast.5) | data formatting | bytes 49152
  88.7 1.3 %copy.14 = f32[5,128]{1,0:T(8,128)} copy(f32[5,128]{1,0:T(8,128)} %get-tuple-element.9) | data formatting | bytes 5120

commit v2 on v1

--- a/solution.py
+++ b/solution.py
@@ -22,20 +22,22 @@
 NCH = NJ // CJ
 NBUF = 6
 N_IND = 8
+LAG = 4
 FAR_FIRST = (6, 2, 5, 7, 4, 1, 3)
 NEAR_FIRST = (1, 3, 4, 5, 7, 2, 6)
 
 
-def far_first(m):
-    return (2 + 3 * m + 3 * (m * (m - 1) // 2)) % 4
+def offset(m):
+    half = m // 2
+    return (1 - m % 2) * 4 + (2 + 3 * half + 3 * (half * (half - 1) // 2)) % 4
 
 
 def kernel(
     g_hbm, r_hbm, places, eff_in, prior, noise, rows, rows_v, gauss,
     out_r, out_eff,
-    wide, stage, r, eff, prefix, norm_prefix, part, spots, table, fix,
-    norm_part, norm_span, factors, changes,
-    core_send, core_recv, far_send, far_recv, norm_recv, ind_recv,
+    wide, stage, r, eff, prefix, norm_prefix, part, table, fix,
+    norm_part, norm_span, factors,
+    mine_send, core_recv, far_send, far_recv, norm_recv, ind_recv,
     load_sem, in_sem, core_ss, core_rs, far_ss, far_rs, ag_ss, ag_rs, fw_ss, fw_rs, nrm_ss, nrm_rs, ind_ss, ind_rs,
 ):
     ind, var = lax.axis_index("ind"), lax.axis_index("var")
@@ -63,7 +65,7 @@
         return pltpu.make_async_copy(g_hbm.at[:, pl.ds(at, CJ * 1024)], stage.at[slot], load_sem.at[slot])
 
     def core_copy(o):
-        return remote(core_send.at[o], core_recv.at[o], core_ss.at[o], core_rs.at[o], (ind, partner))
+        return remote(mine_send.at[o, 1 - core], core_recv.at[o], core_ss.at[o], core_rs.at[o], (ind, partner))
 
     def far_copy(o):
         return remote(
@@ -128,15 +130,15 @@
 
             def widen(jj, norm):
                 sums = [norm[a * 16 : (a + 1) * 16] for a in range(8)]
-                for t in range(8):
-                    at = pl.multiple_of(jj * 1024 + t * 128, 128)
-                    for a in range(8):
+                for a in range(8):
+                    for t in range(8):
+                        at = pl.multiple_of(jj * 1024 + t * 128, 128)
                         v = stage[slot, a * 16 : (a + 1) * 16, pl.ds(at, 128)].astype(F32)
                         wide_rows[pl.ds((c * CJ + jj) * (ROWS * 8) + a * 128 + t, 16, stride=8), :] = v
                         sums[a] = sums[a] + v * v
                 return jnp.concatenate(sums, axis=0)
 
-            norm = lax.fori_loop(0, CJ, widen, norm)
+            norm = lax.fori_loop(0, CJ, widen, norm, unroll=True)
 
             @pl.when(c + NBUF < NCH)
             def _():
@@ -147,18 +149,13 @@
 
     norm_all = lax.fori_loop(0, NS, load, jnp.zeros((ROWS, 128), F32))
 
-    def pick_row(k, width):
-        return (lax.broadcasted_iota(jnp.int32, (8, width), 0) == k).astype(F32)
-
     contract_last = (((1,), (1,)), ((), ()))
 
     def lane_sums(values):
-        total = jnp.zeros((8, values[0].shape[0]), F32)
-        for k in range(K):
-            total = total + lax.dot_general(
-                pick_row(k, 128), values[k], contract_last, precision=HIGHEST, preferred_element_type=F32
-            )
-        return total
+        return jnp.sum(values.T, axis=0, keepdims=True)
+
+    def message(lines):
+        return jnp.concatenate(lines + [jnp.zeros((8 - len(lines), 128), F32)], axis=0)
 
     norm_span[K - 1] = jnp.zeros((ROWS, 128), F32)
 
@@ -173,55 +170,52 @@
                 for t in range(CJ):
                     v = tile(c * CJ + t, a * 8 + i)
                     total = total + jnp.where(keep[t], v * v, 0.0)
-                norm_part[i * 8 : (i + 1) * 8, :] = total
+                norm_part[a % 4, i * 8 : (i + 1) * 8, :] = total
             at = pl.ds(pl.multiple_of(a * 8, 8), 8)
             here = norm_prefix[c, at, :]
             for sub in range(8):
-                here = here + norm_part[pl.ds(sub, 8, stride=8), :]
+                here = here + norm_part[a % 4, pl.ds(sub, 8, stride=8), :]
             norm_span[b, at, :] = here - norm_span[K - 1, at, :]
             norm_span[K - 1, at, :] = here
             return carry
 
-        return lax.fori_loop(0, ROWS // 8, some_rows, carry)
+        return lax.fori_loop(0, ROWS // 8, some_rows, carry, unroll=4)
 
     lax.fori_loop(0, K - 1, norm_below, 0)
-    norm_recv[ind] = lane_sums([norm_span[k] for k in range(K - 1)] + [norm_all - norm_span[K - 1]])
+    norm_recv[ind] = message(
+        [lane_sums(norm_span[k]) for k in range(K - 1)] + [lane_sums(norm_all - norm_span[K - 1])]
+    )
     pl.semaphore_wait(barrier, 15)
     for o in range(1, N_IND):
         norm_copy(o).start()
 
     def send_scores(s):
-        spots[...] = jnp.zeros_like(spots)
-
-        def below(b, carry):
-            q = places[24 + b]
+        slices = [places[24 + b] for b in range(K - 1)]
+        held = []
+        for b in range(K - 1):
             p = places[28 + b]
-            held = []
-            for t in range(TJ):
-                held.append(jnp.where(t * 1024 + place < p, r[q * TJ + t], 0.0))
-            for c in range(BV):
-                row = rows[s, c]
-                total = prefix[q, c]
+            held.append([jnp.where(t * 1024 + place < p, r[slices[b] * TJ + t], 0.0) for t in range(TJ)])
+        for c in range(BV):
+            row = rows[s, c]
+            below = [jnp.zeros((8, 128), F32)]
+            for b in range(K - 1):
+                total = prefix[slices[b], c]
                 for t in range(TJ):
-                    total = total + held[t] * tile(q * TJ + t, row)
-                part[pl.ds(pl.multiple_of((b * BV + c) * 8, 8), 8), :] = total - spots[c]
-                spots[c] = total
-            return carry
-
-        lax.fori_loop(0, K - 1, below, 0)
-        for c in range(BV):
-            at = ((K - 1) * BV + c) * 8
-            part[at : at + 8, :] = prefix[NS, c] - spots[c]
-        values = []
+                    total = total + held[b][t] * tile(slices[b] * TJ + t, row)
+                below.append(total)
+            below.append(prefix[NS, c])
+            for k in range(K):
+                part[(k * BV + c) * 8 : (k * BV + c + 1) * 8, :] = below[k + 1] - below[k]
+        groups = []
         for k in range(K):
-            groups = []
             for a in range(BV // 8):
                 total = part[pl.ds((k * BV + a * 8) * 8, 8, stride=8), :]
                 for sub in range(1, 8):
                     total = total + part[pl.ds((k * BV + a * 8) * 8 + sub, 8, stride=8), :]
                 groups.append(total)
-            values.append(jnp.concatenate(groups, axis=0))
-        ind_recv[s, ind] = jnp.concatenate([lane_sums(values), jnp.zeros((8, 128 - BV), F32)], axis=1)
+        most = lane_sums(jnp.concatenate(groups[: 128 // 8], axis=0))
+        last = lane_sums(jnp.concatenate(groups[128 // 8 :], axis=0))
+        ind_recv[s, ind] = message([most, jnp.concatenate([last, jnp.zeros((1, 128 - BV), F32)], axis=1)])
         for o in range(1, N_IND):
             ind_copy(s, o).start()
 
@@ -274,7 +268,7 @@
         scores = ind_recv[s, 0]
         for other in range(1, N_IND):
             scores = scores + ind_recv[s, other]
-        scores = scores[:, 0:BV]
+        scores = [scores[0:1, k * BV : (k + 1) * BV] for k in range(K - 1)] + [scores[1:2, 0:BV]]
 
         def lower(a, b):
             return factors[s, entry(a, b) : entry(a, b) + 1, :]
@@ -282,10 +276,10 @@
         forward = []
         for a in range(K):
             norm = factors[s, n_entries + a : n_entries + a + 1, :]
-            total = (scores[a : a + 1] + norm * before[a : a + 1]) * inverse[a]
+            total = (scores[a] + norm * before[a : a + 1]) * inverse[a]
             for m in range(a):
                 total = total - lower(a, m) * forward[m]
-            forward.append(total * lower(a, a) + gauss[s, a : a + 1, :])
+            forward.append(total * lower(a, a) + gauss[a, pl.ds(s, 1), :])
         drawn = [None] * K
         for a in reversed(range(K)):
             total = forward[a]
@@ -294,68 +288,65 @@
             drawn[a] = total * lower(a, a)
         rest = jnp.zeros((8 - K, BV), F32)
         change = jnp.concatenate([drawn[k] - before[k : k + 1] for k in range(K)] + [rest], axis=0)
-        changes[...] = change
-
-        def splat(k, carry):
-            line = changes[pl.ds(k, 1), :]
+
+        for k in range(K):
             for c in range(BV):
-                table[k * BV + c] = jnp.broadcast_to(line[:, c : c + 1], (8, 128))
-            return carry
-
-        lax.fori_loop(0, K, splat, 0)
+                table[k * BV + c] = jnp.broadcast_to(change[k : k + 1, c : c + 1], (8, 128))
         eff[...] = eff[...] + lax.dot_general(
             change, chosen, contract_last, precision=HIGHEST, preferred_element_type=F32
         )
 
-        def fixes(b, carry):
-            q = places[24 + b]
+        slices = [places[24 + b] for b in range(K - 1)]
+        totals = [[jnp.zeros((8, 128), F32)] * TJ for b in range(K - 1)]
+        for c in range(BV):
+            row = rows[s, c]
+            low = table[c]
+            for b in range(K - 1):
+                high = table[(b + 1) * BV + c]
+                for t in range(TJ):
+                    totals[b][t] = totals[b][t] + (high - low) * tile(slices[b] * TJ + t, row)
+                low = high
+        for b in range(K - 1):
             p = places[32 + b]
-            totals = [jnp.zeros((8, 128), F32)] * TJ
-            for c in range(BV):
-                row = rows[s, c]
-                more = table[(b + 1) * BV + c] - table[b * BV + c]
-                for t in range(TJ):
-                    totals[t] = totals[t] + more * tile(q * TJ + t, row)
             for t in range(TJ):
-                fix[b, t] = jnp.where(t * 1024 + place >= p, totals[t], 0.0)
-            return carry
-
-        lax.fori_loop(0, K - 1, fixes, 0)
+                fix[b, t] = jnp.where(t * 1024 + place >= p, totals[b][t], 0.0)
 
         def spread(n, carry):
-            half, m = n // 8, n % 8
-            o = (1 - m % 2) * 4 + far_first(m // 2)
-            q = chip_at(o, 1) * 2 + core * half + (1 - core) * (1 - half)
-            k = places[q]
-            totals = [jnp.zeros((8, 128), F32)] * TJ
-            for c in range(BV):
-                row = rows[s, c]
-                factor_c = table[k * BV + c]
-                for t in range(TJ):
-                    totals[t] = totals[t] + factor_c * tile(q * TJ + t, row)
-            for b in range(K - 1):
-                here = jnp.full((8, 128), places[24 + b], jnp.int32) == q
-                for t in range(TJ):
-                    totals[t] = totals[t] + jnp.where(here, fix[b, t], 0.0)
-            mine = jnp.stack(totals)
-
             @pl.when(n < 8)
             def _():
-                core_send[o] = mine
+                o = offset(n)
+                q = chip_at(o, 1) * 2
+                both = [[jnp.zeros((8, 128), F32)] * TJ for half in range(2)]
+                first = [places[q + half] * BV for half in range(2)]
+                for c in range(BV):
+                    row = rows[s, c]
+                    for half in range(2):
+                        factor_c = table[first[half] + c]
+                        for t in range(TJ):
+                            both[half][t] = both[half][t] + factor_c * tile((q + half) * TJ + t, row)
+                for b in range(K - 1):
+                    at = jnp.full((8, 128), places[24 + b], jnp.int32)
+                    for t in range(TJ):
+                        more = fix[b, t]
+                        for half in range(2):
+                            both[half][t] = both[half][t] + jnp.where(at == q + half, more, 0.0)
+                for half in range(2):
+                    mine_send[o, half] = jnp.stack(both[half])
                 core_copy(o).start()
 
-            @pl.when(n >= 8)
+            @pl.when(n >= LAG)
             def _():
+                o = offset(n - LAG)
                 core_copy(o).wait_recv()
-                far_send[o] = mine + core_recv[o]
-
-                @pl.when(n < 15)
+                far_send[o] = mine_send[o, core] + core_recv[o]
+
+                @pl.when(n < LAG + 7)
                 def _():
                     far_copy(o).start()
 
             return carry
 
-        lax.fori_loop(0, 16, spread, 0)
+        lax.fori_loop(0, 8 + LAG, spread, 0)
         mine = far_send[0]
         for o in NEAR_FIRST:
             far_copy(o).wait_recv()
@@ -367,6 +358,7 @@
         def _():
             for o in FAR_FIRST:
                 gather_copy(o).start()
+
             forward_copy(0).start()
             for o in NEAR_FIRST:
                 gather_copy(o).wait_recv()
@@ -417,6 +409,11 @@
         places[24 + b] = q
         places[28 + b] = inside
         places[32 + b] = jnp.where(inside > 0, inside, TJ * 1024)
+
+
+def hand_over(new, new_effects, out_r, out_eff):
+    out_r[...] = new[...]
+    out_eff[...] = new_effects[...]
 
 
 def per_device(genotypes, residual, ancestry, effects, prior_precision, noise_var, block_index, gaussians):
@@ -445,14 +442,12 @@
             pltpu.VMEM((NS + 1, BV, 8, 128), F32),
             pltpu.VMEM((NCH, ROWS, 128), F32),
             pltpu.VMEM((K * BV * 8, 128), F32),
-            pltpu.VMEM((BV, 8, 128), F32),
             pltpu.VMEM((K * BV, 8, 128), F32),
             pltpu.VMEM((K - 1, TJ, 8, 128), F32),
-            pltpu.VMEM((64, 128), F32),
+            pltpu.VMEM((4, 64, 128), F32),
             pltpu.VMEM((K, ROWS, 128), F32),
             pltpu.VMEM((STEPS, 24, BV), F32),
-            pltpu.VMEM((8, BV), F32),
-            pltpu.VMEM((8, TJ, 8, 128), F32),
+            pltpu.VMEM((8, 2, TJ, 8, 128), F32),
             pltpu.VMEM((8, TJ, 8, 128), F32),
             pltpu.VMEM((8, TJ, 8, 128), F32),
             pltpu.VMEM((8, TJ, 8, 128), F32),
@@ -485,8 +480,15 @@
         noise_var,
         block_index,
         block_index,
-        gaussians,
+        gaussians.transpose(1, 0, 2),
     )
+    new, new_effects = pl.pallas_call(
+        hand_over,
+        name="hand_over",
+        out_shape=(jax.ShapeDtypeStruct((TJ, 8, 128), F32), jax.ShapeDtypeStruct((K, ROWS), F32)),
+        in_specs=[whole, whole],
+        out_specs=(whole, whole),
+    )(new, new_effects)
     return new.reshape(-1), new_effects
 
 

time: 90.3 us -> 79.9 us (0.88)
  Pallas kernels: 85.4 us -> 79 us
  local copies, waits for them, and re-layouts: 3.92 us -> 0 us
    pallas_call x1, Pallas kernels: 83.4 us -> 75.7 us  [per_device(): pl.pallas_call(kernel, name='gibbs', out_shape=(jax.ShapeDtypeStruct((TJ,...]
    unnamed x3 -> x0, local copies, waits for them, and re-layouts: 3.92 us -> none
    pallas_call x0 -> x1, Pallas kernels: none -> 1.35 us  [per_device(): pl.pallas_call(hand_over, name='hand_over', out_shape=(jax.ShapeDtypeStru...]
where the time goes in v2:
time: 79.9 us; the launch traced here: 79.6 us
  Pallas kernels  79 us (99%)
    pallas_call x1, Pallas kernels, per_device(): pl.pallas_call(kernel, name='gibbs', out_shape=(jax.ShapeDtypeStruct((TJ,...  75.7 us
    pallas_call x1, Pallas kernels, per_device(): pl.pallas_call(find_places, name='find_places', out_shape=jax.ShapeDtypeS...  1.93 us

profile of v2, /device:TPU:1, one launch (start us, length us, event | category | flops | bytes accessed | tf_op | source)
XLA Modules:
  0.0 79.6 jit_solution(9318694810341233817)
XLA Ops:
  0.6 1.9 %find_places.1.places = s32[36]{0:T(128)} custom-call(s32[96,8,128]{2,1,0:T(8,128)} %bitcast.4), custom_call_target="tpu_custom_call" | custom-call | tf_op jit(solution)/shard_map/find_places/pallas_call | solution.py:424
  2.6 75.7 %gibbs.1 = (f32[6,8,128]{2,1,0:T(8,128)}, f32[5,128]{1,0:T(8,128)}) custom-call(bf16[128,98304]{1,0:T(8,128)(2,1)} %g_hbm.1, f32[96,8,128]{2,1,0:T(8,128)} %bitcast.5, s32[36]{0:T(128)} %find_places.1.places, f32[5,128]{1,0:T(8,128)} %eff_in.1, f32[5,5]{1,0:T(8,128)} %prior.1, f32[5]{0:T(128)} %noise.1, s32[3,32]{1,0:T(4,128)} %rows_v.1, s32[3,32]{1,0:T(4,128)} %rows_v.1, ...), custom_call_target="tpu_custom_call" | custom-call | tf_op jit(solution)/shard_map/gibbs/pallas_call | solution.py:431
  78.3 1.4 %hand_over.1 = (f32[6,8,128]{2,1,0:T(8,128)}, f32[5,128]{1,0:T(8,128)}) custom-call(f32[6,8,128]{2,1,0:T(8,128)} %get-tuple-element.6.new, f32[5,128]{1,0:T(8,128)} %get-tuple-element.7.new_effects), custom_call_target="tpu_custom_call" | custom-call | tf_op jit(solution)/shard_map/hand_over/pallas_call | solution.py:485

commit v3 on v2

--- a/solution.py
+++ b/solution.py
@@ -22,7 +22,6 @@
 NCH = NJ // CJ
 NBUF = 6
 N_IND = 8
-LAG = 4
 FAR_FIRST = (6, 2, 5, 7, 4, 1, 3)
 NEAR_FIRST = (1, 3, 4, 5, 7, 2, 6)
 
@@ -33,9 +32,9 @@
 
 
 def kernel(
-    g_hbm, r_hbm, places, eff_in, prior, noise, rows, rows_v, gauss,
+    g_hbm, r_hbm, anc_hbm, eff_in, prior, noise, rows, rows_v, gauss,
     out_r, out_eff,
-    wide, stage, r, eff, prefix, norm_prefix, part, table, fix,
+    wide, stage, r, anc, eff, prefix, norm_prefix, part, table, fix,
     norm_part, norm_span, factors,
     mine_send, core_recv, far_send, far_recv, norm_recv, ind_recv,
     load_sem, in_sem, core_ss, core_rs, far_ss, far_rs, ag_ss, ag_rs, fw_ss, fw_rs, nrm_ss, nrm_rs, ind_ss, ind_rs,
@@ -86,7 +85,9 @@
     def ind_copy(s, o):
         return remote(ind_recv.at[s, ind], ind_recv.at[s, ind], ind_ss.at[s, o], ind_rs.at[s, o], (ind_at(o), var))
 
-    r_copy = pltpu.make_async_copy(r_hbm, r, in_sem)
+    anc_copy = pltpu.make_async_copy(anc_hbm, anc, in_sem.at[0])
+    r_copy = pltpu.make_async_copy(r_hbm, r, in_sem.at[1])
+    anc_copy.start()
     r_copy.start()
     for c in range(NBUF):
         chunk(c, c).start()
@@ -98,6 +99,18 @@
     for o in range(1, N_IND):
         pl.semaphore_signal(barrier, inc=1, device_id=(ind_at(o), var), device_id_type=MESH)
 
+    anc_copy.wait()
+
+    def count(group, totals):
+        for i in range(8):
+            a = anc[group * 8 + i]
+            totals = tuple(t + (a < b + 1).astype(jnp.int32) for b, t in enumerate(totals))
+        return totals
+
+    totals = lax.fori_loop(0, NJ // 8, count, (jnp.zeros((8, 128), jnp.int32),) * (K - 1))
+    begins = [jnp.sum(t) for t in totals]
+    chunk_of = [jnp.minimum(lax.div(p, CJ * 1024), NCH - 1) for p in begins]
+    slice_of = [jnp.minimum(lax.div(p, TJ * 1024), NS - 1) for p in begins]
     r_copy.wait()
     eff[...] = jnp.zeros_like(eff)
     eff[0:K, :] = eff_in[...]
@@ -159,9 +172,9 @@
 
     norm_span[K - 1] = jnp.zeros((ROWS, 128), F32)
 
-    def norm_below(b, carry):
-        c = places[16 + b]
-        p = places[20 + b]
+    def norm_below(b):
+        c = chunk_of[b]
+        p = begins[b] - c * (CJ * 1024)
         keep = [t * 1024 + place < p for t in range(CJ)]
 
         def some_rows(a, carry):
@@ -179,9 +192,10 @@
             norm_span[K - 1, at, :] = here
             return carry
 
-        return lax.fori_loop(0, ROWS // 8, some_rows, carry, unroll=4)
-
-    lax.fori_loop(0, K - 1, norm_below, 0)
+        lax.fori_loop(0, ROWS // 8, some_rows, 0, unroll=4)
+
+    for b in range(K - 1):
+        norm_below(b)
     norm_recv[ind] = message(
         [lane_sums(norm_span[k]) for k in range(K - 1)] + [lane_sums(norm_all - norm_span[K - 1])]
     )
@@ -190,10 +204,10 @@
         norm_copy(o).start()
 
     def send_scores(s):
-        slices = [places[24 + b] for b in range(K - 1)]
+        slices = slice_of
         held = []
         for b in range(K - 1):
-            p = places[28 + b]
+            p = begins[b] - slices[b] * (TJ * 1024)
             held.append([jnp.where(t * 1024 + place < p, r[slices[b] * TJ + t], 0.0) for t in range(TJ)])
         for c in range(BV):
             row = rows[s, c]
@@ -296,7 +310,7 @@
             change, chosen, contract_last, precision=HIGHEST, preferred_element_type=F32
         )
 
-        slices = [places[24 + b] for b in range(K - 1)]
+        slices = slice_of
         totals = [[jnp.zeros((8, 128), F32)] * TJ for b in range(K - 1)]
         for c in range(BV):
             row = rows[s, c]
@@ -307,46 +321,44 @@
                     totals[b][t] = totals[b][t] + (high - low) * tile(slices[b] * TJ + t, row)
                 low = high
         for b in range(K - 1):
-            p = places[32 + b]
+            p = jnp.full((8, 128), begins[b] - slices[b] * (TJ * 1024), jnp.int32)
             for t in range(TJ):
-                fix[b, t] = jnp.where(t * 1024 + place >= p, totals[b][t], 0.0)
+                fix[b, t] = jnp.where((t * 1024 + place >= p) & (p > 0), totals[b][t], 0.0)
 
         def spread(n, carry):
+            half, m = n // 8, n % 8
+            o = offset(m)
+            q = chip_at(o, 1) * 2 + core * half + (1 - core) * (1 - half)
+            k = sum([(p <= q * (TJ * 1024)).astype(jnp.int32) for p in begins])
+            totals = [jnp.zeros((8, 128), F32)] * TJ
+            for c in range(BV):
+                row = rows[s, c]
+                factor_c = table[k * BV + c]
+                for t in range(TJ):
+                    totals[t] = totals[t] + factor_c * tile(q * TJ + t, row)
+            for b in range(K - 1):
+                here = jnp.full((8, 128), slice_of[b], jnp.int32) == q
+                for t in range(TJ):
+                    totals[t] = totals[t] + jnp.where(here, fix[b, t], 0.0)
+            mine = jnp.stack(totals)
+
             @pl.when(n < 8)
             def _():
-                o = offset(n)
-                q = chip_at(o, 1) * 2
-                both = [[jnp.zeros((8, 128), F32)] * TJ for half in range(2)]
-                first = [places[q + half] * BV for half in range(2)]
-                for c in range(BV):
-                    row = rows[s, c]
-                    for half in range(2):
-                        factor_c = table[first[half] + c]
-                        for t in range(TJ):
-                            both[half][t] = both[half][t] + factor_c * tile((q + half) * TJ + t, row)
-                for b in range(K - 1):
-                    at = jnp.full((8, 128), places[24 + b], jnp.int32)
-                    for t in range(TJ):
-                        more = fix[b, t]
-                        for half in range(2):
-                            both[half][t] = both[half][t] + jnp.where(at == q + half, more, 0.0)
-                for half in range(2):
-                    mine_send[o, half] = jnp.stack(both[half])
+                mine_send[o, 1 - core] = mine
                 core_copy(o).start()
 
-            @pl.when(n >= LAG)
+            @pl.when(n >= 8)
             def _():
-                o = offset(n - LAG)
                 core_copy(o).wait_recv()
-                far_send[o] = mine_send[o, core] + core_recv[o]
-
-                @pl.when(n < LAG + 7)
+                far_send[o] = mine + core_recv[o]
+
+                @pl.when(n < 15)
                 def _():
                     far_copy(o).start()
 
             return carry
 
-        lax.fori_loop(0, 8 + LAG, spread, 0)
+        lax.fori_loop(0, 16, spread, 0)
         mine = far_send[0]
         for o in NEAR_FIRST:
             far_copy(o).wait_recv()
@@ -392,25 +404,6 @@
         norm_copy(o).wait_send()
 
 
-def find_places(anc, places):
-    totals = [jnp.zeros((8, 128), jnp.int32)] * (K - 1)
-    for j in range(NJ):
-        a = anc[j]
-        totals = [t + (a < b + 1).astype(jnp.int32) for b, t in enumerate(totals)]
-    begins = [jnp.sum(t) for t in totals]
-    for q in range(NS):
-        places[q] = sum([(begins[b] <= q * (TJ * 1024)).astype(jnp.int32) for b in range(K - 1)])
-    for b in range(K - 1):
-        c = jnp.minimum(lax.div(begins[b], CJ * 1024), NCH - 1)
-        q = jnp.minimum(lax.div(begins[b], TJ * 1024), NS - 1)
-        inside = begins[b] - q * (TJ * 1024)
-        places[16 + b] = c
-        places[20 + b] = begins[b] - c * (CJ * 1024)
-        places[24 + b] = q
-        places[28 + b] = inside
-        places[32 + b] = jnp.where(inside > 0, inside, TJ * 1024)
-
-
 def hand_over(new, new_effects, out_r, out_eff):
     out_r[...] = new[...]
     out_eff[...] = new_effects[...]
@@ -421,23 +414,17 @@
     scalar = pl.BlockSpec(memory_space=pltpu.SMEM)
     anywhere = pl.BlockSpec(memory_space=pl.ANY)
     dma = pltpu.SemaphoreType.DMA
-    places = pl.pallas_call(
-        find_places,
-        name="find_places",
-        out_shape=jax.ShapeDtypeStruct((36,), jnp.int32),
-        in_specs=[whole],
-        out_specs=scalar,
-    )(ancestry.reshape(NJ, 8, 128))
     new, new_effects = pl.pallas_call(
         kernel,
         name="gibbs",
         out_shape=(jax.ShapeDtypeStruct((TJ, 8, 128), F32), jax.ShapeDtypeStruct((K, ROWS), F32)),
-        in_specs=[anywhere, anywhere, scalar, whole, scalar, scalar, scalar, whole, whole],
+        in_specs=[anywhere, anywhere, anywhere, whole, scalar, scalar, scalar, whole, whole],
         out_specs=(whole, whole),
         scratch_shapes=[
             pltpu.VMEM((NJ * ROWS, 8, 128), F32),
             pltpu.VMEM((NBUF, ROWS, CJ * 1024), jnp.bfloat16),
             pltpu.VMEM((NJ, 8, 128), F32),
+            pltpu.VMEM((NJ, 8, 128), jnp.int32),
             pltpu.VMEM((8, ROWS), F32),
             pltpu.VMEM((NS + 1, BV, 8, 128), F32),
             pltpu.VMEM((NCH, ROWS, 128), F32),
@@ -454,7 +441,7 @@
             pltpu.VMEM((N_IND, 8, 128), F32),
             pltpu.VMEM((STEPS, N_IND, 8, 128), F32),
             dma((NBUF,)),
-            dma,
+            dma((2,)),
             dma((8,)),
             dma((8,)),
             dma((8,)),
@@ -474,7 +461,7 @@
     )(
         genotypes,
         residual.reshape(NJ, 8, 128),
-        places,
+        ancestry.reshape(NJ, 8, 128),
         effects,
         prior_precision,
         noise_var,

time: 79.9 us -> 77.4 us (0.969)
  Pallas kernels: 79 us -> 76.5 us
    pallas_call x1 -> x0, Pallas kernels: 1.93 us -> none  [per_device(): pl.pallas_call(find_places, name='find_places', out_shape=jax.ShapeDtypeS...]
where the time goes in v3:
time: 77.4 us; the launch traced here: 77.1 us
  Pallas kernels  76.5 us (99%)
    pallas_call x1, Pallas kernels, per_device(): pl.pallas_call(kernel, name='gibbs', out_shape=(jax.ShapeDtypeStruct((TJ,...  75.1 us

profile of v3, /device:TPU:1, one launch (start us, length us, event | category | flops | bytes accessed | tf_op | source)
XLA Modules:
  0.0 77.1 jit_solution(12195191427459533125)
XLA Ops:
  0.6 75.1 %gibbs.1 = (f32[6,8,128]{2,1,0:T(8,128)}, f32[5,128]{1,0:T(8,128)}) custom-call(bf16[128,98304]{1,0:T(8,128)(2,1)} %g_hbm.1, f32[96,8,128]{2,1,0:T(8,128)} %bitcast.4, s32[96,8,128]{2,1,0:T(8,128)} %bitcast.5, f32[5,128]{1,0:T(8,128)} %eff_in.1, f32[5,5]{1,0:T(8,128)} %prior.1, f32[5]{0:T(128)} %noise.1, s32[3,32]{1,0:T(4,128)} %rows_v.1, s32[3,32]{1,0:T(4,128)} %rows_v.1, ...), custom_call_target="tpu_custom_call" | custom-call | tf_op jit(solution)/shard_map/gibbs/pallas_call | solution.py:417
  75.8 1.4 %hand_over.1 = (f32[6,8,128]{2,1,0:T(8,128)}, f32[5,128]{1,0:T(8,128)}) custom-call(f32[6,8,128]{2,1,0:T(8,128)} %get-tuple-element.6.new, f32[5,128]{1,0:T(8,128)} %get-tuple-element.7.new_effects), custom_call_target="tpu_custom_call" | custom-call | tf_op jit(solution)/shard_map/hand_over/pallas_call | solution.py:472

commit v4 on v3

--- a/solution.py
+++ b/solution.py
@@ -24,6 +24,7 @@
 N_IND = 8
 FAR_FIRST = (6, 2, 5, 7, 4, 1, 3)
 NEAR_FIRST = (1, 3, 4, 5, 7, 2, 6)
+IND_FAR_FIRST = (6, 5, 7, 2, 4, 1, 3)
 
 
 def offset(m):
@@ -200,7 +201,7 @@
         [lane_sums(norm_span[k]) for k in range(K - 1)] + [lane_sums(norm_all - norm_span[K - 1])]
     )
     pl.semaphore_wait(barrier, 15)
-    for o in range(1, N_IND):
+    for o in IND_FAR_FIRST:
         norm_copy(o).start()
 
     def send_scores(s):
@@ -230,7 +231,7 @@
         most = lane_sums(jnp.concatenate(groups[: 128 // 8], axis=0))
         last = lane_sums(jnp.concatenate(groups[128 // 8 :], axis=0))
         ind_recv[s, ind] = message([most, jnp.concatenate([last, jnp.zeros((1, 128 - BV), F32)], axis=1)])
-        for o in range(1, N_IND):
+        for o in IND_FAR_FIRST:
             ind_copy(s, o).start()
 
     send_scores(0)

time: 77.4 us -> 77.2 us (level)
  no operation moved by 1% of the time
where the time goes in v4:
time: 77.2 us; the launch traced here: 77 us
  Pallas kernels  76.3 us (99%)
    pallas_call x1, Pallas kernels, per_device(): pl.pallas_call(kernel, name='gibbs', out_shape=(jax.ShapeDtypeStruct((TJ,...  75 us

profile of v4, /device:TPU:1, one launch (start us, length us, event | category | flops | bytes accessed | tf_op | source)
XLA Modules:
  0.0 77.0 jit_solution(16560848522297541880)
XLA Ops:
  0.6 75.0 %gibbs.1 = (f32[6,8,128]{2,1,0:T(8,128)}, f32[5,128]{1,0:T(8,128)}) custom-call(bf16[128,98304]{1,0:T(8,128)(2,1)} %g_hbm.1, f32[96,8,128]{2,1,0:T(8,128)} %bitcast.4, s32[96,8,128]{2,1,0:T(8,128)} %bitcast.5, f32[5,128]{1,0:T(8,128)} %eff_in.1, f32[5,5]{1,0:T(8,128)} %prior.1, f32[5]{0:T(128)} %noise.1, s32[3,32]{1,0:T(4,128)} %rows_v.1, s32[3,32]{1,0:T(4,128)} %rows_v.1, ...), custom_call_target="tpu_custom_call" | custom-call | tf_op jit(solution)/shard_map/gibbs/pallas_call | solution.py:418
  75.6 1.4 %hand_over.1 = (f32[6,8,128]{2,1,0:T(8,128)}, f32[5,128]{1,0:T(8,128)}) custom-call(f32[6,8,128]{2,1,0:T(8,128)} %get-tuple-element.6.new, f32[5,128]{1,0:T(8,128)} %get-tuple-element.7.new_effects), custom_call_target="tpu_custom_call" | custom-call | tf_op jit(solution)/shard_map/hand_over/pallas_call | solution.py:473
